TPU v7x, 32 devices: a whole 2x2x4 slice. The times are simulated.
32 devices in a mesh: groups: 2 (over y), ckpt: 4 (over z), hid: 4 (over x, core).
Axes of the slice: x: 2, y: 2, z: 4, core: 2. Of those that a mesh axis runs over, the one named last changes fastest.
Arguments:
- residual_stream: bfloat16 [4, 768, 2048], P('ckpt', ('groups', 'hid')), parts along dimension 1, may hold values from -6 to 6
- norm_gain: float32 [4, 2048], P('ckpt'), may hold values from 0.1 to 1.9
- norm_shift: float32 [4, 2048], P('ckpt'), may hold values from -3 to 3
- input_weight: bfloat16 [4, 2048, 4096], P('ckpt', None, 'hid'), may hold values from -0.125 to 0.125
- input_bias: float32 [4, 4096], P('ckpt', 'hid'), may hold values from -3 to 3
- output_weight: bfloat16 [4, 4096, 2048], P('ckpt', 'hid'), may hold values from -0.09375 to 0.09375
- output_bias: float32 [4, 2048], P('ckpt'), may hold values from -3 to 3
- encoder_weight: bfloat16 [4, 2048, 4096], P('ckpt', None, 'hid'), may hold values from -0.0625 to 0.0625
- encoder_bias: float32 [4096], P('hid'), may hold values from -3 to 3
- decoder_weight: bfloat16 [4, 4096, 2048], P('ckpt', None, 'hid'), may hold values from -0.09375 to 0.09375
- decoder_bias: float32 [4, 2048], P('ckpt', 'hid'), may hold values from -3 to 3
Outputs:
- latent_codes: bfloat16 [768, 4096], P('groups', 'hid'), parts along dimension 0
- recon_error: float32 [4, 768, 2048], P('ckpt', 'groups', 'hid'), parts along dimension 1
There are 2 independent parts, one for each index of `groups`. A program takes and returns all parts, laid end to end along the dimension named above; an argument that names none is the same for every part. Nothing has to cross between parts.
All inputs are finite; a program needn't handle non-finite values.
Results may differ from a plain program's by a relative error of at most 0.0056.
Values may be sent and summed in bfloat16 or wider, within the bound.
A program may use at most 64 MiB of HBM per device.

v0:
```python
import jax
import jax.numpy as jnp
from jax import lax
from jax.sharding import PartitionSpec as P


def per_device(
    residual_stream,
    norm_gain,
    norm_shift,
    input_weight,
    input_bias,
    output_weight,
    output_bias,
    encoder_weight,
    encoder_bias,
    decoder_weight,
    decoder_bias,
):
    values = residual_stream[0].astype(jnp.float32)
    average = jnp.mean(values, axis=-1, keepdims=True)
    centred = values - average
    variance = jnp.mean(centred * centred, axis=-1, keepdims=True)
    normed = (centred * lax.rsqrt(variance + 1e-05) * norm_gain[0] + norm_shift[0]).astype(
        jnp.bfloat16
    )
    first_weight = input_weight[0]
    first_bias = input_bias[0]
    second_weight = output_weight[0]
    hidden = jax.nn.gelu(
        jnp.dot(
            lax.all_gather(normed, "hid", axis=0, tiled=True),
            first_weight,
            preferred_element_type=jnp.float32,
        )
        + first_bias,
        approximate=False,
    ).astype(jnp.bfloat16)
    partial_out = jnp.dot(hidden, second_weight, preferred_element_type=jnp.float32)
    mlp_out = (lax.psum(partial_out, "hid") + output_bias[0]).astype(jnp.bfloat16)
    encoder_terms = jnp.dot(mlp_out, encoder_weight[0], preferred_element_type=jnp.float32)
    latent_codes = jax.nn.relu(lax.psum(encoder_terms, "ckpt") + encoder_bias).astype(jnp.bfloat16)
    local_decoder = decoder_weight[0]
    column_count = local_decoder.shape[1]
    rebuilt = (
        jnp.dot(
            lax.all_gather(latent_codes, "hid", axis=1, tiled=True),
            local_decoder,
            preferred_element_type=jnp.float32,
        )
        + decoder_bias[0]
    )
    own_columns = lax.dynamic_slice_in_dim(
        mlp_out, lax.axis_index("hid") * column_count, column_count, 1
    ).astype(jnp.float32)
    recon_error = (own_columns - rebuilt)[None]
    return (latent_codes, recon_error)


def solution(mesh):
    placed = (
        P("ckpt", ("groups", "hid"), None),
        P("ckpt", None),
        P("ckpt", None),
        P("ckpt", None, "hid"),
        P("ckpt", "hid"),
        P("ckpt", "hid", None),
        P("ckpt", None),
        P("ckpt", None, "hid"),
        P("hid"),
        P("ckpt", None, "hid"),
        P("ckpt", "hid"),
    )
    return jax.shard_map(
        per_device,
        mesh=mesh,
        in_specs=placed,
        out_specs=(P("groups", "hid"), P("ckpt", "groups", "hid")),
        check_vma=False,
    )
```

profile of v0, /device:TPU:1, one launch (start us, length us, event | category | flops | bytes accessed | tf_op | source)
XLA Modules:
  0.0 233.0 jit_solution(14858888776073998837)
XLA Ops:
  7.2 0.0 copy-start.3
  7.2 0.0 all-gather.3.cloned.1.call-start
  7.2 1.1 convert_reduce_fusion
  8.4 1.3 fusion.34
  9.7 2.1 fusion.37
  11.7 0.0 all-gather.3.cloned.1.call-update
  11.8 0.0 all-reduce.3.cloned.1.call-start
  11.8 22.2 %all-gather.3.cloned.1.call-done = bf16[384,2048]{1,0:T(8,128)(2,1)} async-done(((bf16[96,2048]{1,0:T(8,128)(2,1)}), bf16[384,2048]{1,0:T(8,128)(2,1)}) %all-gather.3.cloned.1.call-update) | async-done | bytes 1572880 | tf_op jit(solution)/shard_map/all_gather | solution.py:32
  34.1 0.0 copy-done.3
  34.1 12.3 %fusion.4 = f32[384,2048]{1,0:T(8,128)} fusion(bf16[1,1024,2048]{2,1,0:T(8,128)(2,1)} %param.16, bf16[384,2048]{1,0:T(8,128)(2,1)} %all-gather.3.cloned.1.call-done, bf16[1,2048,1024]{2,1,0:T(8,128)(2,1)} %param.14, f32[1024]{0:T(1024)S(1)} %bitcast.51), kind=kOutput, calls=%fused_computation.4 | convolution fusion | flops 3247177728 | bytes 13111296 | tf_op jit(solution)/shard_map/dot_general | solution.py:39
  46.3 0.0 copy-start
  46.3 0.0 all-reduce.3.cloned.1.call-update
  46.3 0.0 all-reduce.5.cloned.1.call-start
  46.4 68.0 %all-reduce.3.cloned.1.call-done = f32[384,2048]{1,0:T(8,128)} async-done(((f32[384,2048]{1,0:T(8,128)}), f32[384,2048]{1,0:T(8,128)}) %all-reduce.3.cloned.1.call-update) | async-done | bytes 3145744 | tf_op jit(solution)/shard_map/psum | solution.py:40
  114.4 0.0 copy-done
  114.4 0.0 copy-start.2
  114.4 2.4 %add_convert_fusion = bf16[384,2048]{1,0:T(8,128)(2,1)S(1)} fusion(f32[384,2048]{1,0:T(8,128)} %all-reduce.3.cloned.1.call-done, f32[2048]{0:T(1024)S(1)} %bitcast.50), kind=kLoop, calls=%fused_computation.8 | loop fusion | flops 1572864 | bytes 4726784 | tf_op jit(solution)/shard_map/convert_element_type | solution.py:40
  116.8 0.8 copy-done.2
  117.6 3.0 %fusion.2 = f32[384,1024]{1,0:T(8,128)} fusion(bf16[384,2048]{1,0:T(8,128)(2,1)S(1)} %add_convert_fusion, bf16[1,2048,1024]{2,1,0:T(8,128)(2,1)S(1)} %copy-done.2), kind=kOutput, calls=%fused_computation.2 | convolution fusion | flops 1610612736 | bytes 7340032 | tf_op jit(solution)/shard_map/dot_general | solution.py:41
  120.5 0.0 copy-start.1
  120.5 0.0 all-reduce.5.cloned.1.call-update
  120.6 0.0 copy-start.4
  120.6 0.0 all-gather.5.cloned.1.call-start
  120.6 68.3 %all-reduce.5.cloned.1.call-done = f32[384,1024]{1,0:T(8,128)} async-done(((f32[384,1024]{1,0:T(8,128)}), f32[384,1024]{1,0:T(8,128)}) %all-reduce.5.cloned.1.call-update) | async-done | bytes 1572880 | tf_op jit(solution)/shard_map/psum | solution.py:42
  188.9 0.0 copy-done.1
  188.9 2.5 %maximum_convert_fusion = bf16[384,1024]{1,0:T(8,128)(2,1)} fusion(f32[384,1024]{1,0:T(8,128)} %all-reduce.5.cloned.1.call-done, f32[1024]{0:T(1024)S(1)} %copy-done.1), kind=kLoop, calls=%fused_computation.13 | loop fusion | flops 1179648 | bytes 2363392 | tf_op jit(solution)/shard_map/convert_element_type | solution.py:42
  191.4 0.0 all-gather.5.cloned.1.call-update
  191.4 29.3 %all-gather.5.cloned.1.call-done = bf16[384,4096]{1,0:T(8,128)(2,1)} async-done(((bf16[384,1024]{1,0:T(8,128)(2,1)}), bf16[384,4096]{1,0:T(8,128)(2,1)}) %all-gather.5.cloned.1.call-update) | async-done | bytes 3145744 | tf_op jit(solution)/shard_map/all_gather | solution.py:47
  220.7 0.0 copy-done.4
  220.7 5.8 %fusion.26 = f32[1,384,512]{2,1,0:T(8,128)} fusion(bf16[384,4096]{1,0:T(8,128)(2,1)} %all-gather.5.cloned.1.call-done, bf16[1,4096,512]{2,1,0:T(8,128)(2,1)} %param.20, f32[512]{0:T(512)S(1)} %bitcast.52, bf16[384,2048]{1,0:T(8,128)(2,1)S(1)} %add_convert_fusion, s32[]{:T(128)S(6)} %select_n.3), kind=kOutput, calls=%fused_computation.31 | convolution fusion | flops 1611202560 | bytes 8521732 | tf_op jit(solution)/shard_map/dot_general | solution.py:46
  (2 shorter events, 0.0 us)
Async XLA Ops:
  7.2 26.9 %copy-start.3 = (f32[1,1024]{1,0:T(1,128)S(1)}, f32[1,1024]{1,0:T(1,128)}, u32[]{:S(2)}) copy-start(f32[1,1024]{1,0:T(1,128)} %param.15) | copy-start | bytes 12292
  7.2 26.9 %all-gather.3.cloned.1.call-start = ((), (), s32[]{:S(2)}) async-start(), calls=%async_computation | async-start | bytes 1966080 | tf_op jit(solution)/shard_map/all_gather | solution.py:32
  11.8 102.7 %all-reduce.3.cloned.1.call-start = ((), (), s32[]{:S(2)}) async-start(), calls=%async_computation.1 | async-start | bytes 6291456 | tf_op jit(solution)/shard_map/psum | solution.py:40
  46.3 68.1 %copy-start = (f32[1,2048]{1,0:T(1,128)S(1)}, f32[1,2048]{1,0:T(1,128)}, u32[]{:S(2)}) copy-start(f32[1,2048]{1,0:T(1,128)} %param.17) | copy-start | bytes 24580
  46.3 142.6 %all-reduce.5.cloned.1.call-start = ((), (), s32[]{:S(2)}) async-start(), calls=%async_computation.2 | async-start | bytes 3145728 | tf_op jit(solution)/shard_map/psum | solution.py:42
  114.4 3.1 %copy-start.2 = (bf16[1,2048,1024]{2,1,0:T(8,128)(2,1)S(1)}, bf16[1,2048,1024]{2,1,0:T(8,128)(2,1)}, u32[]{:S(2)}) copy-start(bf16[1,2048,1024]{2,1,0:T(8,128)(2,1)} %param.18) | copy-start | bytes 12582916
  120.5 68.4 %copy-start.1 = (f32[1024]{0:T(1024)S(1)}, f32[1024]{0:T(1024)}, u32[]{:S(2)}) copy-start(f32[1024]{0:T(1024)} %param.19) | copy-start | bytes 12292
  120.6 100.1 %copy-start.4 = (f32[1,512]{1,0:T(1,128)S(1)}, f32[1,512]{1,0:T(1,128)}, u32[]{:S(2)}) copy-start(f32[1,512]{1,0:T(1,128)} %param.21) | copy-start | bytes 6148
  120.6 100.1 %all-gather.5.cloned.1.call-start = ((), (), s32[]{:S(2)}) async-start(), calls=%async_computation.3 | async-start | bytes 3932160 | tf_op jit(solution)/shard_map/all_gather | solution.py:47
Sparse Core Ops, SparseCore 0:
  11.9 22.1 all-gather.2
  46.5 67.9 all-reduce.2
  120.7 68.2 all-reduce.4
  191.6 29.0 all-gather.4
where the time goes:
time: 233 us
  waiting for transfers between devices  188 us (81%)
  matrix products  21 us (9%)
  between operations  13.8 us (6%)
  other arithmetic  9.33 us (4%)
    psum x1, waiting for transfers between devices, per_device(): lax.psum(encoder_terms, 'ckpt') + encoder_bias  68.3 us
    psum x1, waiting for transfers between devices, per_device(): lax.psum(partial_out, 'hid') + output_bias[0]  68 us
    all_gather x1, waiting for transfers between devices, per_device(): lax.all_gather(latent_codes, 'hid', axis=1, tiled=True)  29.3 us
    all_gather x1, waiting for transfers between devices, per_device(): lax.all_gather(normed, 'hid', axis=0, tiled=True)  22.2 us
    dot_general x1, matrix products, per_device(): jnp.dot(hidden, second_weight, preferred_element_type=jnp.float32)  12.3 us
    dot_general x1, matrix products, per_device(): jnp.dot(lax.all_gather(latent_codes, 'hid', axis=1, tiled=True), local_de...  5.81 us
  transfers between devices with their start and end apart: 4, of which 4 were waited for; matrix products, arithmetic and copies ran while one was open for 0% of the time, Pallas kernels for 0%

commit v1 on v0

--- a/solution.py
+++ b/solution.py
@@ -1,10 +1,14 @@
+import functools
+
 import jax
 import jax.numpy as jnp
 from jax import lax
+from jax.experimental import pallas as pl
+from jax.experimental.pallas import tpu as pltpu
 from jax.sharding import PartitionSpec as P
 
 
-def per_device(
+def with_collectives(
     residual_stream,
     norm_gain,
     norm_shift,
@@ -57,7 +61,312 @@
     return (latent_codes, recon_error)
 
 
+CHUNKS = 2
+F32, BF16 = jnp.float32, jnp.bfloat16
+
+
+def kernel(
+    n, res, gain, shift, b1, b2, be, bd, w1_hbm, w2_hbm, we_hbm, wd_hbm, codes_out, recon_out,
+    w1, w2, we, wd, nbuf, hbuf, psend, precv, pown, xsend, xrecv, mbuf, pre, zsend, zrecv, cbuf, obuf,
+    sw, sa, ra, sb, rb, sx, rx, sm, rm, sz, rz, sc, rc, sd, rd, se, re, so,
+):
+    K = CHUNKS
+    S = nbuf.shape[2]
+    M = n * S
+    D = nbuf.shape[3]
+    FFL = w1.shape[1]
+    LATL = we.shape[1]
+    TW = D // n
+    T = n // 2
+    NX = n // 2
+    NZ = n
+    h = lax.axis_index("hid")
+    z = lax.axis_index("ckpt")
+    c = lax.rem(h, 2)
+    sib = h + 1 - 2 * c
+    sends = []
+
+    def hpeer(j):
+        return lax.rem(h + 2 * j, n)
+
+    def hfrom(j):
+        return lax.rem(h + n - 2 * j, n)
+
+    def zpeer(j):
+        return lax.rem(z + j, NZ)
+
+    def zfrom(j):
+        return lax.rem(z + NZ - j, NZ)
+
+    def remote(src, dst, ssem, rsem, **dev):
+        return pltpu.make_async_remote_copy(
+            src_ref=src, dst_ref=dst, send_sem=ssem, recv_sem=rsem,
+            device_id=dev, device_id_type=pl.DeviceIdType.MESH,
+        )
+
+    def send(src, dst, ssem, rsem, **dev):
+        copy = remote(src, dst, ssem, rsem, **dev)
+        copy.start()
+        sends.append(copy)
+
+    def arrived(dst, ssem, rsem):
+        remote(dst, dst, ssem, rsem, hid=sib).wait_recv()
+
+    loads = [
+        pltpu.make_async_copy(a, b, sw.at[i])
+        for i, (a, b) in enumerate(((w1_hbm, w1), (w2_hbm, w2), (we_hbm, we), (wd_hbm, wd)))
+    ]
+    for load in loads:
+        load.start()
+
+    barrier = pltpu.get_barrier_semaphore()
+    peers = [dict(hid=sib)] + [dict(hid=hpeer(j)) for j in range(1, NX)]
+    peers += [dict(ckpt=zpeer(j)) for j in range(1, NZ)]
+    for dev in peers:
+        pl.semaphore_signal(barrier, inc=1, device_id=dev, device_id_type=pl.DeviceIdType.MESH)
+
+    def normalise(k):
+        values = res[k * S : (k + 1) * S, :].astype(F32)
+        average = jnp.mean(values, axis=-1, keepdims=True)
+        centred = values - average
+        variance = jnp.mean(centred * centred, axis=-1, keepdims=True)
+        nbuf[k, h] = (centred * lax.rsqrt(variance + 1e-05) * gain[...] + shift[...]).astype(BF16)
+
+    def spread(k):
+        for j in range(1, NX):
+            send(nbuf.at[k, h], nbuf.at[k, h], sa.at[k, 1, j], ra.at[k, h], hid=hpeer(j))
+        send(nbuf.at[k, h], nbuf.at[k, h], sa.at[k, 0, 0], ra.at[k, h], hid=sib)
+
+    def relay(k):
+        for j in range(1, NX):
+            o = hfrom(j)
+            arrived(nbuf.at[k, o], sa.at[k, 0, 0], ra.at[k, o])
+            send(nbuf.at[k, o], nbuf.at[k, o], sa.at[k, 0, j], ra.at[k, o], hid=sib)
+
+    def first(k):
+        arrived(nbuf.at[k, sib], sa.at[k, 0, 0], ra.at[k, sib])
+        for j in range(1, NX):
+            o = lax.rem(sib + n - 2 * j, n)
+            arrived(nbuf.at[k, o], sa.at[k, 0, 0], ra.at[k, o])
+        if k == 0:
+            loads[0].wait()
+
+        def tile(i, _):
+            cols = pl.ds(pl.multiple_of(i * 256, 256), 256)
+            u = jnp.dot(nbuf[k].reshape(M, D), w1[:, cols], preferred_element_type=F32) + b1[:, cols]
+            hbuf[:, cols] = (0.5 * u * (1.0 + lax.erf(u * 0.7071067811865476))).astype(BF16)
+            return 0
+
+        lax.fori_loop(0, FFL // 256, tile, 0)
+
+    def project(g):
+        cols = pl.ds(pl.multiple_of(g * TW, TW), TW)
+        return jnp.dot(hbuf[...], w2[:, cols], preferred_element_type=F32)
+
+    def second(k, between):
+        if k == 0:
+            loads[1].wait()
+        for t in range(T):
+            psend[k, t] = project((1 - c) * T + t).astype(BF16)
+            send(psend.at[k, t], precv.at[k, t], sb.at[k, t], rb.at[k, t], hid=sib)
+        between()
+        for t in range(T):
+            own = project(c * T + t)
+            arrived(precv.at[k, t], sb.at[k, t], rb.at[k, t])
+            own = own + precv[k, t].astype(F32)
+            pown[k, t] = own
+            xsend[k, t] = own.astype(BF16)
+            for j in range(1, NX):
+                send(xsend.at[k, t], xrecv.at[k, t, j], sx.at[k, t, j], rx.at[k, t, j], hid=hpeer(j))
+
+    def encode(k, g, start):
+        rows = pl.ds(pl.multiple_of(g * TW, TW), TW)
+
+        def tile(i, _):
+            cols = pl.ds(pl.multiple_of(i * 256, 256), 256)
+            u = jnp.dot(mbuf[k, g], we[rows, cols], preferred_element_type=F32)
+            pre[k, :, cols] = u if start else pre[k, :, cols] + u
+            return 0
+
+        lax.fori_loop(0, LATL // 256, tile, 0)
+
+    def finish(k):
+        for t in range(T):
+            g = c * T + t
+            total = pown[k, t]
+            for j in range(1, NX):
+                arrived(xrecv.at[k, t, j], sx.at[k, t, j], rx.at[k, t, j])
+                total = total + xrecv[k, t, j].astype(F32)
+            mbuf[k, g] = (total + b2[:, pl.ds(pl.multiple_of(g * TW, TW), TW)]).astype(BF16)
+            send(mbuf.at[k, g], mbuf.at[k, g], sm.at[k, t], rm.at[k, t], hid=sib)
+            if k == 0 and t == 0:
+                loads[2].wait()
+            encode(k, g, t == 0)
+        for t in range(T):
+            g = (1 - c) * T + t
+            arrived(mbuf.at[k, g], sm.at[k, t], rm.at[k, t])
+            encode(k, g, False)
+        for j in range(1, NZ):
+            b = zpeer(j)
+            zsend[k, j] = pre[k, pl.ds(pl.multiple_of(b * S, S), S), :].astype(BF16)
+            send(zsend.at[k, j], zrecv.at[k, j], sz.at[k, j], rz.at[k, j], ckpt=b)
+
+    def codes(k):
+        total = pre[k, pl.ds(pl.multiple_of(z * S, S), S), :]
+        for j in range(1, NZ):
+            arrived(zrecv.at[k, j], sz.at[k, j], rz.at[k, j])
+            total = total + zrecv[k, j].astype(F32)
+        cbuf[k, h, z] = jnp.maximum(total + be[...], 0.0).astype(BF16)
+        for j in range(1, NZ):
+            send(cbuf.at[k, h, z], cbuf.at[k, h, z], sc.at[k, j], rc.at[k, j], ckpt=zpeer(j))
+        across(k, 0)
+
+    def across(k, i):
+        b = zfrom(i)
+        for j in range(1, NX):
+            send(cbuf.at[k, h, b], cbuf.at[k, h, b], sd.at[k, i, j], rd.at[k, b, j], hid=hpeer(j))
+
+    outs = []
+
+    def put(src, dst, sem):
+        copy = pltpu.make_async_copy(src, dst, sem)
+        copy.start()
+        outs.append(copy)
+
+    def collect(k):
+        for i in range(1, NZ):
+            b = zfrom(i)
+            arrived(cbuf.at[k, h, b], sc.at[k, i], rc.at[k, i])
+            across(k, i)
+        send(cbuf.at[k, h], cbuf.at[k, h], se.at[k, 0], re.at[k, 0], hid=sib)
+        for b in range(NZ):
+            put(cbuf.at[k, h, b], codes_out.at[pl.ds((b * K + k) * S, S), :], so.at[0, k, b])
+
+    def decode(k):
+        def part(o):
+            return jnp.dot(
+                cbuf[k, o].reshape(M, LATL),
+                wd[pl.ds(pl.multiple_of(o * LATL, LATL), LATL), :],
+                preferred_element_type=F32,
+            )
+
+        if k == 0:
+            loads[3].wait()
+        obuf[k] = mbuf[k, h].astype(F32) - (part(h) + bd[...])
+        arrived(cbuf.at[k, sib], se.at[k, 0], re.at[k, 0])
+        obuf[k] -= part(sib)
+        for j in range(1, NX):
+            o = hfrom(j)
+            for b in range(NZ):
+                arrived(cbuf.at[k, o, b], sd.at[k, b, j], rd.at[k, b, j])
+            send(cbuf.at[k, o], cbuf.at[k, o], se.at[k, j], re.at[k, j], hid=sib)
+            obuf[k] -= part(o)
+        for j in range(1, NX):
+            o = lax.rem(sib + n - 2 * j, n)
+            arrived(cbuf.at[k, o], se.at[k, j], re.at[k, j])
+            obuf[k] -= part(o)
+        for b in range(NZ):
+            put(obuf.at[k, pl.ds(b * S, S), :], recon_out.at[pl.ds((b * K + k) * S, S), :], so.at[1, k, b])
+
+    normalise(0)
+    pl.semaphore_wait(barrier, len(peers))
+    spread(0)
+    for k in range(1, K):
+        normalise(k)
+        spread(k)
+    relay(0)
+    for k in range(K):
+        first(k)
+        second(k, functools.partial(relay, k + 1) if k + 1 < K else (lambda: None))
+    for k in range(K):
+        finish(k)
+    for k in range(K):
+        codes(k)
+        collect(k)
+    for k in range(K):
+        decode(k)
+    for copy in outs:
+        copy.wait()
+    for copy in sends:
+        copy.wait_send()
+
+
+def fused(res, gain, shift, w1, b1, w2, b2, we, be, wd, bd, hid):
+    K, n = CHUNKS, hid
+    rows, D = res.shape[1:]
+    FFL, LATL, OUTL = w1.shape[2], we.shape[2], wd.shape[2]
+    S = rows // K
+    M = n * S
+    T = NX = n // 2
+    TW = D // n
+    dma = pltpu.SemaphoreType.DMA
+    vmem = pl.BlockSpec(memory_space=pltpu.VMEM)
+    hbm = pl.BlockSpec(memory_space=pl.ANY)
+    codes, recon = pl.pallas_call(
+        functools.partial(kernel, n),
+        out_shape=(
+            jax.ShapeDtypeStruct((n * rows, LATL), BF16),
+            jax.ShapeDtypeStruct((n * rows, OUTL), F32),
+        ),
+        in_specs=[vmem] * 7 + [hbm] * 4,
+        out_specs=(hbm, hbm),
+        scratch_shapes=[
+            pltpu.VMEM(w1.shape[1:], BF16),
+            pltpu.VMEM(w2.shape[1:], BF16),
+            pltpu.VMEM(we.shape[1:], BF16),
+            pltpu.VMEM(wd.shape[1:], BF16),
+            pltpu.VMEM((K, n, S, D), BF16),
+            pltpu.VMEM((M, FFL), BF16),
+            pltpu.VMEM((K, T, M, TW), BF16),
+            pltpu.VMEM((K, T, M, TW), BF16),
+            pltpu.VMEM((K, T, M, TW), F32),
+            pltpu.VMEM((K, T, M, TW), BF16),
+            pltpu.VMEM((K, T, NX, M, TW), BF16),
+            pltpu.VMEM((K, n, M, TW), BF16),
+            pltpu.VMEM((K, M, LATL), F32),
+            pltpu.VMEM((K, n, S, LATL), BF16),
+            pltpu.VMEM((K, n, S, LATL), BF16),
+            pltpu.VMEM((K, n, n, S, LATL), BF16),
+            pltpu.VMEM((K, M, OUTL), F32),
+            dma((4,)),
+            dma((K, 2, NX)),
+            dma((K, n)),
+            dma((K, T)),
+            dma((K, T)),
+            dma((K, T, NX)),
+            dma((K, T, NX)),
+            dma((K, T)),
+            dma((K, T)),
+            dma((K, n)),
+            dma((K, n)),
+            dma((K, n)),
+            dma((K, n)),
+            dma((K, n, NX)),
+            dma((K, n, NX)),
+            dma((K, NX)),
+            dma((K, NX)),
+            dma((2, K, n)),
+        ],
+        compiler_params=pltpu.CompilerParams(
+            collective_id=0, has_side_effects=True, vmem_limit_bytes=56 * 1024 * 1024
+        ),
+    )(
+        res[0], gain, shift, b1, b2, be.reshape(1, LATL), bd,
+        w1[0], w2[0], we[0], wd[0],
+    )
+    return codes, recon[None]
+
+
 def solution(mesh):
+    hid, ckpt = mesh.shape["hid"], mesh.shape["ckpt"]
+
+    def body(*operands):
+        rows, width = operands[0].shape[1:]
+        latents = operands[7].shape[2]
+        fits = hid == ckpt and hid % 2 == 0 and rows % (16 * CHUNKS) == 0
+        fits = fits and latents % 256 == 0 and width % (256 * hid) == 0
+        return (fused if fits and hid <= 4 else with_collectives)(*operands, **(dict(hid=hid) if fits and hid <= 4 else {}))
+
     placed = (
         P("ckpt", ("groups", "hid"), None),
         P("ckpt", None),
@@ -72,7 +381,7 @@
         P("ckpt", "hid"),
     )
     return jax.shard_map(
-        per_device,
+        body,
         mesh=mesh,
         in_specs=placed,
         out_specs=(P("groups", "hid"), P("ckpt", "groups", "hid")),

time: 233 us -> 80.6 us (0.35)
  waiting for transfers between devices: 188 us -> 0 us
  Pallas kernels: 0 us -> 74.3 us
  matrix products: 21 us -> 0 us
  between operations: 13.8 us -> 0.64 us
  other arithmetic: 9.33 us -> 0 us
  local copies, waits for them, and re-layouts: 0.78 us -> 4.13 us
    psum x2 -> x0, waiting for transfers between devices: 136 us -> none  [the longest x1 68.3 us: per_device(): lax.psum(encoder_terms, 'ckpt') + encoder_bias]
    pallas_call x0 -> x1, Pallas kernels: none -> 74.3 us  [fused(): pl.pallas_call(functools.partial(kernel, n), out_shape=(jax.ShapeDtypeStr...]
    all_gather x2 -> x0, waiting for transfers between devices: 51.5 us -> none  [the longest x1 29.3 us: per_device(): lax.all_gather(latent_codes, 'hid', axis=1, tiled=True)]
    dot_general x3 -> x0, matrix products: 21 us -> none  [the longest x1 12.3 us: per_device(): jnp.dot(hidden, second_weight, preferred_element_type=jnp.float32)]
    convert_element_type x3 -> x0, other arithmetic: 6.91 us -> none  [the longest x1 2.47 us: per_device(): jax.nn.relu(lax.psum(encoder_terms, 'ckpt') + encoder_bias)]
    unnamed x10 -> x2, local copies, waits for them, and re-layouts: 0.78 us -> 4.13 us
    reduce_sum x2 -> x0, other arithmetic: 2.42 us -> none  [the longest x1 1.27 us: per_device(): variance = jnp.mean(centred * centred, axis=-1, keepdims=True)]
  transfers between devices with their start and end apart: 4 -> 0, of which waited for: 4 -> 0; matrix products, arithmetic and copies ran while one was open for 0% -> 0% of each run, Pallas kernels for 0% -> 0%
where the time goes in v1:
time: 80.6 us; the launch traced here: 79.1 us
  Pallas kernels  74.3 us (92%)
  local copies, waits for them, and re-layouts  4.13 us (5%)
    pallas_call x1, Pallas kernels, fused(): pl.pallas_call(functools.partial(kernel, n), out_shape=(jax.ShapeDtypeStr...  74.3 us
    unnamed x2, local copies, waits for them, and re-layouts  4.13 us

profile of v1, /device:TPU:1, one launch (start us, length us, event | category | flops | bytes accessed | tf_op | source)
XLA Modules:
  0.0 79.1 jit_solution(5755397897367874109)
XLA Ops:
  0.6 74.3 %shard_map.122 = (bf16[384,1024]{1,0:T(8,128)(2,1)}, f32[384,512]{1,0:T(8,128)}) custom-call(bf16[96,2048]{1,0:T(8,128)(2,1)} %bitcast.12, f32[1,2048]{1,0:T(1,128)} %gain.1, f32[1,2048]{1,0:T(1,128)} %shift.1, f32[1,1024]{1,0:T(1,128)} %b1.1, f32[1,2048]{1,0:T(1,128)} %b2.1, f32[1,1024]{1,0:T(1,128)} %bitcast.13, f32[1,512]{1,0:T(1,128)} %bd.1, ...), custom_call_target="tpu_custom_call" | custom-call | tf_op jit(solution)/shard_map/pallas_call | solution.py:305
  75.0 2.1 %copy.15 = bf16[384,1024]{1,0:T(8,128)(2,1)} copy(bf16[384,1024]{1,0:T(8,128)(2,1)} %get-tuple-element.8) | data formatting | bytes 1572864
  77.0 2.1 %copy.16 = f32[1,384,512]{2,1,0:T(8,128)} copy(f32[1,384,512]{2,1,0:T(8,128)} %bitcast.11) | data formatting | bytes 1572864

commit v2 on v1

--- a/solution.py
+++ b/solution.py
@@ -61,7 +61,7 @@
     return (latent_codes, recon_error)
 
 
-CHUNKS = 2
+CHUNKS = 3
 F32, BF16 = jnp.float32, jnp.bfloat16
 
 
@@ -217,14 +217,30 @@
             arrived(zrecv.at[k, j], sz.at[k, j], rz.at[k, j])
             total = total + zrecv[k, j].astype(F32)
         cbuf[k, h, z] = jnp.maximum(total + be[...], 0.0).astype(BF16)
-        for j in range(1, NZ):
-            send(cbuf.at[k, h, z], cbuf.at[k, h, z], sc.at[k, j], rc.at[k, j], ckpt=zpeer(j))
-        across(k, 0)
-
-    def across(k, i):
-        b = zfrom(i)
-        for j in range(1, NX):
-            send(cbuf.at[k, h, b], cbuf.at[k, h, b], sd.at[k, i, j], rd.at[k, b, j], hid=hpeer(j))
+        pl.when(z < NZ - 1)(passing(k, z, 1).start)
+        pl.when(z > 0)(passing(k, z, 0).start)
+        over(k, z)
+
+    def passing(k, b, up):
+        there = jnp.minimum(z + 1, NZ - 1) if up else jnp.maximum(z - 1, 0)
+        block = cbuf.at[k, h, b]
+        return remote(block, block, sc.at[k, up, b], rc.at[k, b], ckpt=there)
+
+    def over(k, b):
+        for j in range(1, NX):
+            crossing(k, b, j).start()
+
+    def crossing(k, b, j):
+        block = cbuf.at[k, h, b]
+        return remote(block, block, sd.at[k, b, j], rd.at[k, b, j], hid=hpeer(j))
+
+    def passed():
+        for k in range(K):
+            for b in range(NZ):
+                pl.when(jnp.logical_and(b <= z, z < NZ - 1))(passing(k, b, 1).wait_send)
+                pl.when(jnp.logical_and(b >= z, z > 0))(passing(k, b, 0).wait_send)
+                for j in range(1, NX):
+                    crossing(k, b, j).wait_send()
 
     outs = []
 
@@ -235,9 +251,20 @@
 
     def collect(k):
         for i in range(1, NZ):
-            b = zfrom(i)
-            arrived(cbuf.at[k, h, b], sc.at[k, i], rc.at[k, i])
-            across(k, i)
+            @pl.when(z - i >= 0)
+            def _():
+                b = z - i
+                arrived(cbuf.at[k, h, b], sc.at[k, 0, b], rc.at[k, b])
+                pl.when(z < NZ - 1)(passing(k, b, 1).start)
+                over(k, b)
+
+            @pl.when(z + i < NZ)
+            def _():
+                b = z + i
+                arrived(cbuf.at[k, h, b], sc.at[k, 0, b], rc.at[k, b])
+                pl.when(z > 0)(passing(k, b, 0).start)
+                over(k, b)
+
         send(cbuf.at[k, h], cbuf.at[k, h], se.at[k, 0], re.at[k, 0], hid=sib)
         for b in range(NZ):
             put(cbuf.at[k, h, b], codes_out.at[pl.ds((b * K + k) * S, S), :], so.at[0, k, b])
@@ -274,21 +301,49 @@
     for k in range(1, K):
         normalise(k)
         spread(k)
-    relay(0)
-    for k in range(K):
+    def mlp(k):
         first(k)
         second(k, functools.partial(relay, k + 1) if k + 1 < K else (lambda: None))
-    for k in range(K):
-        finish(k)
-    for k in range(K):
-        codes(k)
-        collect(k)
-    for k in range(K):
-        decode(k)
+
+    relay(0)
+    mlp(0)
+    mlp(1)
+    finish(0)
+    mlp(2)
+    finish(1)
+    codes(0)
+    finish(2)
+    codes(1)
+    collect(0)
+    codes(2)
+    collect(1)
+    decode(0)
+    collect(2)
+    decode(1)
+    decode(2)
     for copy in outs:
         copy.wait()
     for copy in sends:
         copy.wait_send()
+    passed()
+
+
+def landing(codes, recon, codes_out, recon_out):
+    codes_out[...] = codes[...]
+    recon_out[...] = recon[...]
+
+
+def land(codes, recon):
+    vmem = pl.BlockSpec(memory_space=pltpu.VMEM)
+    return pl.pallas_call(
+        landing,
+        out_shape=(
+            jax.ShapeDtypeStruct(codes.shape, codes.dtype),
+            jax.ShapeDtypeStruct(recon.shape, recon.dtype),
+        ),
+        in_specs=[vmem] * 2,
+        out_specs=(vmem, vmem),
+    )(codes, recon)
 
 
 def fused(res, gain, shift, w1, b1, w2, b2, we, be, wd, bd, hid):
@@ -339,7 +394,7 @@
             dma((K, T)),
             dma((K, n)),
             dma((K, n)),
-            dma((K, n)),
+            dma((K, 2, n)),
             dma((K, n)),
             dma((K, n, NX)),
             dma((K, n, NX)),
@@ -354,7 +409,7 @@
         res[0], gain, shift, b1, b2, be.reshape(1, LATL), bd,
         w1[0], w2[0], we[0], wd[0],
     )
-    return codes, recon[None]
+    return land(codes, recon[None])
 
 
 def solution(mesh):

time: 80.6 us -> 75.1 us (0.932); the launches traced: 79.1 us -> 74.9 us
  local copies, waits for them, and re-layouts: 4.13 us -> 0 us
    unnamed x2 -> x0, local copies, waits for them, and re-layouts: 4.13 us -> none
    pallas_call x1, Pallas kernels: 74.3 us -> 71.7 us  [fused(): pl.pallas_call(functools.partial(kernel, n), out_shape=(jax.ShapeDtypeStr...]
    pallas_call x0 -> x1, Pallas kernels: none -> 2.56 us  [land(): pl.pallas_call(landing, out_shape=(jax.ShapeDtypeStruct(codes.shape, code...]
where the time goes in v2:
time: 75.1 us; the launch traced here: 74.9 us
  Pallas kernels  74.3 us (99%)
    pallas_call x1, Pallas kernels, fused(): pl.pallas_call(functools.partial(kernel, n), out_shape=(jax.ShapeDtypeStr...  71.7 us
    pallas_call x1, Pallas kernels, land(): pl.pallas_call(landing, out_shape=(jax.ShapeDtypeStruct(codes.shape, code...  2.56 us

profile of v2, /device:TPU:1, one launch (start us, length us, event | category | flops | bytes accessed | tf_op | source)
XLA Modules:
  0.0 74.9 jit_solution(18181332883559392720)
XLA Ops:
  0.6 71.7 %shard_map.122 = (bf16[384,1024]{1,0:T(8,128)(2,1)}, f32[384,512]{1,0:T(8,128)}) custom-call(bf16[96,2048]{1,0:T(8,128)(2,1)} %bitcast.12, f32[1,2048]{1,0:T(1,128)} %gain.1, f32[1,2048]{1,0:T(1,128)} %shift.1, f32[1,1024]{1,0:T(1,128)} %b1.1, f32[1,2048]{1,0:T(1,128)} %b2.1, f32[1,1024]{1,0:T(1,128)} %bitcast.13, f32[1,512]{1,0:T(1,128)} %bd.1, ...), custom_call_target="tpu_custom_call" | custom-call | tf_op jit(solution)/shard_map/pallas_call | solution.py:360
  72.4 2.6 %shard_map.123 = (bf16[384,1024]{1,0:T(8,128)(2,1)}, f32[1,384,512]{2,1,0:T(8,128)}) custom-call(bf16[384,1024]{1,0:T(8,128)(2,1)} %get-tuple-element.4.codes, f32[1,384,512]{2,1,0:T(8,128)} %bitcast.11), custom_call_target="tpu_custom_call" | custom-call | tf_op jit(solution)/shard_map/pallas_call | solution.py:338

commit v3 on v2

--- a/solution.py
+++ b/solution.py
@@ -301,15 +301,17 @@
     for k in range(1, K):
         normalise(k)
         spread(k)
-    def mlp(k):
-        first(k)
+    def later(k):
         second(k, functools.partial(relay, k + 1) if k + 1 < K else (lambda: None))
 
     relay(0)
-    mlp(0)
-    mlp(1)
+    first(0)
+    later(0)
+    first(1)
+    later(1)
+    first(2)
     finish(0)
-    mlp(2)
+    later(2)
     finish(1)
     codes(0)
     finish(2)

time: 75.1 us -> 73.7 us (0.981)
  Pallas kernels: 74.3 us -> 72.9 us
    pallas_call x1, Pallas kernels: 71.7 us -> 70.3 us  [fused(): pl.pallas_call(functools.partial(kernel, n), out_shape=(jax.ShapeDtypeStr...]
where the time goes in v3:
time: 73.7 us; the launch traced here: 73.5 us
  Pallas kernels  72.9 us (99%)
    pallas_call x1, Pallas kernels, fused(): pl.pallas_call(functools.partial(kernel, n), out_shape=(jax.ShapeDtypeStr...  70.3 us
    pallas_call x1, Pallas kernels, land(): pl.pallas_call(landing, out_shape=(jax.ShapeDtypeStruct(codes.shape, code...  2.56 us

profile of v3, /device:TPU:1, one launch (start us, length us, event | category | flops | bytes accessed | tf_op | source)
XLA Modules:
  0.0 73.5 jit_solution(17554468372017692554)
XLA Ops:
  0.6 70.3 %shard_map.122 = (bf16[384,1024]{1,0:T(8,128)(2,1)}, f32[384,512]{1,0:T(8,128)}) custom-call(bf16[96,2048]{1,0:T(8,128)(2,1)} %bitcast.12, f32[1,2048]{1,0:T(1,128)} %gain.1, f32[1,2048]{1,0:T(1,128)} %shift.1, f32[1,1024]{1,0:T(1,128)} %b1.1, f32[1,2048]{1,0:T(1,128)} %b2.1, f32[1,1024]{1,0:T(1,128)} %bitcast.13, f32[1,512]{1,0:T(1,128)} %bd.1, ...), custom_call_target="tpu_custom_call" | custom-call | tf_op jit(solution)/shard_map/pallas_call | solution.py:362
  71.0 2.6 %shard_map.123 = (bf16[384,1024]{1,0:T(8,128)(2,1)}, f32[1,384,512]{2,1,0:T(8,128)}) custom-call(bf16[384,1024]{1,0:T(8,128)(2,1)} %get-tuple-element.4.codes, f32[1,384,512]{2,1,0:T(8,128)} %bitcast.11), custom_call_target="tpu_custom_call" | custom-call | tf_op jit(solution)/shard_map/pallas_call | solution.py:340
